TPU v7x, 32 devices: a whole 2x2x4 slice. The times are simulated.
32 devices in a mesh: section: 2 (over x), expert: 16 (over z, y, core).
Axes of the slice: x: 2, y: 2, z: 4, core: 2. Of those that a mesh axis runs over, the one named last changes fastest.
Arguments:
- tokens: bfloat16 [384, 7168], P('expert', 'section'), may hold values from -6 to 6
- expert_ids: int32 [384, 8], P('expert'), may hold values from 0 to 15, all different within a row; in each aligned block of 24 rows (0 to 23, 24 to 47, ...) at most 16 rows name the same one
- gate_weights: bfloat16 [384, 8], P('expert'), may hold values from 0.099609375 to 0.59765625
- w_gate: bfloat16 [16, 1024, 7168], P('expert', 'section'), may hold values from -0.0625 to 0.0625
- w_up: bfloat16 [16, 1024, 7168], P('expert', 'section'), may hold values from -0.0625 to 0.0625
- w_down: bfloat16 [16, 1024, 7168], P('expert', 'section'), may hold values from -0.1875 to 0.1875
Outputs:
- mixed: bfloat16 [384, 7168], P('expert', 'section')
Inputs may be any that keep to these rules, and one draw needn't show every extreme that they name: `expert_ids`: in each aligned block of 24 rows (the rows of one device), no expert is named by more than 16 of the block's pairs, a bound that some block reaches; a row names 8 different experts.
All inputs are finite; a program needn't handle non-finite values.
Results may differ from a plain program's by a relative error of at most 0.0057.
Values may be sent and summed in bfloat16 or wider, within the bound.
A program may use at most 128 MiB of HBM per device.

v0:
```python
import jax
import jax.numpy as jnp
from jax import lax
from jax.sharding import PartitionSpec as P


def on_device(tokens, expert_ids, gate_weights, w_gate, w_up, w_down):
    n_dest = lax.axis_size("expert")
    token_count = tokens.shape[0]
    chosen = expert_ids.shape[1]
    width = w_gate.shape[2]
    capacity = min(token_count, token_count * chosen * 4 // (3 * n_dest))
    flat_ids = expert_ids.reshape(-1)
    onehot = (flat_ids[:, None] == jnp.arange(n_dest, dtype=jnp.int32)[None, :]).astype(jnp.int32)
    order_rank = jnp.cumsum(onehot, axis=0) - 1
    slot_index = jnp.sum(order_rank * onehot, axis=1)
    target = flat_ids * capacity + slot_index
    token_of = jnp.arange(token_count * chosen, dtype=jnp.int32) // chosen
    matches = (jnp.arange(n_dest * capacity, dtype=jnp.int32)[:, None] == target[None, :]).astype(
        jnp.bfloat16
    )
    token_map = (token_of[:, None] == jnp.arange(token_count, dtype=jnp.int32)[None, :]).astype(
        jnp.bfloat16
    )
    dispatch_matrix = jnp.dot(matches, token_map, preferred_element_type=jnp.float32).astype(
        jnp.bfloat16
    )
    scaled_map = token_map * gate_weights.reshape(-1)[:, None]
    combine_matrix = jnp.dot(scaled_map.T, matches.T, preferred_element_type=jnp.float32).astype(
        jnp.bfloat16
    )
    contract_last = (((1,), (1,)), ((), ()))
    features = lax.all_gather(tokens, "section", axis=1, tiled=True)
    send_rows = jnp.dot(dispatch_matrix, features, preferred_element_type=jnp.float32).astype(
        jnp.bfloat16
    )
    send_rows = send_rows.reshape(n_dest, capacity, width)
    received = lax.all_to_all(send_rows, "expert", split_axis=0, concat_axis=0, tiled=True)
    inputs = received.reshape(-1, width)
    gated = lax.dot_general(inputs, w_gate[0], contract_last, preferred_element_type=jnp.float32)
    upward = lax.dot_general(inputs, w_up[0], contract_last, preferred_element_type=jnp.float32)
    hidden = (jax.nn.silu(gated) * upward).astype(jnp.bfloat16)
    partial_value = jnp.dot(hidden, w_down[0], preferred_element_type=jnp.float32).astype(
        jnp.bfloat16
    )
    partial_value = partial_value.reshape((received.shape[0], received.shape[1], width))
    returned = lax.all_to_all(partial_value, "expert", split_axis=0, concat_axis=0, tiled=True)
    weighted = jnp.dot(
        combine_matrix, returned.reshape(-1, width), preferred_element_type=jnp.float32
    )
    return lax.psum_scatter(weighted, "section", scatter_dimension=1, tiled=True).astype(
        jnp.bfloat16
    )


def solution(mesh):
    placed = (
        P("expert", "section"),
        P("expert", None),
        P("expert", None),
        P("expert", "section", None),
        P("expert", "section", None),
        P("expert", "section", None),
    )
    return jax.shard_map(
        on_device, mesh=mesh, in_specs=placed, out_specs=P("expert", "section"), check_vma=False
    )
```

profile of v0, /device:TPU:13, one launch (start us, length us, event | category | flops | bytes accessed | tf_op | source)
XLA Modules:
  0.0 237.3 jit_solution(17440436958217824420)
XLA Ops:
  6.5 0.8 copy.8
  7.3 0.1 reshape.49
  7.4 0.6 reduce-window.6
  8.0 0.2 slice_reduce_fusion
  8.2 0.1 bitcast_bitcast_fusion
  8.3 6.1 %all_gather.3 = bf16[24,7168]{1,0:T(8,128)(2,1)S(1)} all-gather(bf16[24,3584]{1,0:T(8,128)(2,1)} %param.6), channel_id=1, replica_groups=mesh['section'=2,'expert'=16] {'section'}, dimensions={1}, use_global_device_ids=true | all-gather | bytes 516096 | tf_op jit(solution)/shard_map/all_gather | solution.py:33
  14.5 3.2 %convolution_convert_fusion.1 = bf16[256,7168]{1,0:T(8,128)(2,1)} fusion(bf16[24,7168]{1,0:T(8,128)(2,1)S(1)} %all_gather.3, s32[192]{0:T(256)S(1)} %get-tuple-element.6, s32[192]{0:T(256)S(1)} %get-tuple-element.5), kind=kOutput, calls=%fused_computation.1 | convolution fusion | flops 92334592 | bytes 4015616 | tf_op jit(solution)/shard_map/dot_general | solution.py:34
  17.6 0.0 copy-start.2
  17.6 88.7 %all_to_all.10 = bf16[16,16,7168]{2,1,0:T(8,128)(2,1)S(1)} all-to-all(bf16[16,16,7168]{2,1,0:T(8,128)(2,1)} %bitcast.35), channel_id=1, replica_groups=mesh['section'=2,'expert'=16] {'expert'}, dimensions={0} | all-to-all | bytes 7340032 | tf_op jit(solution)/shard_map/all_to_all | solution.py:38
  106.3 0.0 copy-start
  106.3 1.8 copy-done
  108.1 0.0 copy-done.2
  108.1 2.1 fusion.3
  110.2 12.2 %convolution_convert_fusion = bf16[256,7168]{1,0:T(8,128)(2,1)} fusion(bf16[1,512,7168]{2,1,0:T(8,128)(2,1)} %param.11, bf16[256,7168]{1,0:T(8,128)(2,1)} %bitcast.38, bf16[1,512,7168]{2,1,0:T(8,128)(2,1)} %param.10, f32[256,512]{1,0:T(8,128)S(1)} %fusion.3), kind=kOutput, calls=%fused_computation | convolution fusion | flops 3760717824 | bytes 22544384 | tf_op jit(solution)/shard_map/dot_general | solution.py:43
  122.4 0.0 copy-start.1
  122.4 5.4 %all-to-all-start.1 = ((bf16[16,16,7168]{2,1,0:T(8,128)(2,1)}), bf16[16,16,7168]{2,1,0:T(8,128)(2,1)}, u32[]{:S(2)}, u32[]{:S(2)}) async-start(bf16[16,16,7168]{2,1,0:T(8,128)(2,1)} %bitcast.36), calls=%async_computation.1 | async-start | bytes 7340032 | tf_op jit(solution)/shard_map/all_to_all | solution.py:47
  127.8 0.0 reduce-scatter.2.cloned.1.call-start
  127.8 0.0 copy-done.1
  127.8 0.1 copy.7
  127.9 0.1 mul.30
  128.0 81.0 %all-to-all-done.1 = bf16[16,16,7168]{2,1,0:T(8,128)(2,1)} async-done(((bf16[16,16,7168]{2,1,0:T(8,128)(2,1)}), bf16[16,16,7168]{2,1,0:T(8,128)(2,1)}, u32[]{:S(2)}, u32[]{:S(2)}) %all-to-all-start.1) | async-done | bytes 3670048 | tf_op jit(solution)/shard_map/all_to_all | solution.py:47
  209.0 3.8 %fusion.11 = f32[24,7168]{1,0:T(8,128)} fusion(bf16[256,7168]{1,0:T(8,128)(2,1)} %bitcast.7, s32[192]{0:T(256)S(1)} %get-tuple-element.6, s32[192]{0:T(256)S(1)} %get-tuple-element.5, bf16[192]{0:T(256)(128)(2,1)S(1)} %mul.30), kind=kOutput, calls=%fused_computation.11 | convolution fusion | flops 90504192 | bytes 4360064 | tf_op jit(solution)/shard_map/dot_general | solution.py:48
  212.8 0.0 reduce-scatter.2.cloned.1.call-update
  212.8 16.0 %reduce-scatter.2.cloned.1.call-done = f32[24,3584]{1,0:T(8,128)} async-done(((f32[24,7168]{1,0:T(8,128)}), f32[24,3584]{1,0:T(8,128)}) %reduce-scatter.2.cloned.1.call-update) | async-done | bytes 344080 | tf_op jit(solution)/shard_map/reduce_scatter | solution.py:51
  228.8 1.7 convert_element_type.27
  (6 shorter events, 0.1 us)
Async XLA Ops:
  17.6 90.5 %copy-start.2 = (bf16[1,512,7168]{2,1,0:T(8,128)(2,1)S(1)}, bf16[1,512,7168]{2,1,0:T(8,128)(2,1)}, u32[]{:S(2)}) copy-start(bf16[1,512,7168]{2,1,0:T(8,128)(2,1)} %param.9) | copy-start | bytes 22020100
  106.3 1.8 copy-start
  122.4 5.4 %copy-start.1 = (bf16[24,8]{0,1:T(8,128)(2,1)S(1)}, bf16[24,8]{0,1:T(8,128)(2,1)}, u32[]{:S(2)}) copy-start(bf16[24,8]{0,1:T(8,128)(2,1)} %param.8) | copy-start | bytes 1156
  122.4 86.6 %all-to-all-start.1 = ((bf16[16,16,7168]{2,1,0:T(8,128)(2,1)}), bf16[16,16,7168]{2,1,0:T(8,128)(2,1)}, u32[]{:S(2)}, u32[]{:S(2)}) async-start(bf16[16,16,7168]{2,1,0:T(8,128)(2,1)} %bitcast.36), calls=%async_computation.1 | async-start | bytes 7340032 | tf_op jit(solution)/shard_map/all_to_all | solution.py:47
  127.8 101.0 %reduce-scatter.2.cloned.1.call-start = ((), (), s32[]{:S(2)}) async-start(), calls=%async_computation.3 | async-start | bytes 1032192 | tf_op jit(solution)/shard_map/reduce_scatter | solution.py:51
Sparse Core Ops, SparseCore 0:
  212.9 15.7 reduce-scatter.1
where the time goes:
time: 239 us; the launch traced here: 237 us
  waiting for transfers between devices  97 us (41%)
  blocking collectives  94.8 us (40%)
  matrix products  21.2 us (9%)
  between operations  13.5 us (6%)
  starting transfers between devices  5.41 us (2%)
  local copies, waits for them, and re-layouts  3.02 us (1%)
  other arithmetic  2.41 us (1%)
    all_to_all x1, blocking collectives, on_device(): lax.all_to_all(send_rows, 'expert', split_axis=0, concat_axis=0, tiled=True)  88.7 us
    all_to_all x1, waiting for transfers between devices, on_device(): lax.all_to_all(partial_value, 'expert', split_axis=0, concat_axis=0, tile...  81 us
    reduce_scatter x1, waiting for transfers between devices, on_device(): lax.psum_scatter(weighted, 'section', scatter_dimension=1, tiled=True)  16 us
    dot_general x1, matrix products, on_device(): jnp.dot(hidden, w_down[0], preferred_element_type=jnp.float32)  12.2 us
    all_gather x1, blocking collectives, on_device(): features = lax.all_gather(tokens, 'section', axis=1, tiled=True)  6.13 us
    all_to_all x1, starting transfers between devices, on_device(): lax.all_to_all(partial_value, 'expert', split_axis=0, concat_axis=0, tile...  5.37 us
  transfers between devices with their start and end apart: 2, of which 2 were waited for; matrix products, arithmetic and copies ran while one was open for 0% of the time, Pallas kernels for 0%

commit v1 on v0

v1 whole, which is shorter than its diff:
```python
import jax
import jax.numpy as jnp
from jax import lax
from jax.sharding import PartitionSpec as P


def on_device(tokens, expert_ids, gate_weights, w_gate, w_up, w_down):
    me = lax.axis_index("expert")
    contract_last = (((1,), (1,)), ((), ()))
    rows = lax.all_gather(tokens, "section", axis=1, tiled=True)
    inputs = lax.all_gather(rows, "expert", axis=0, tiled=True)
    ids = lax.all_gather(expert_ids, "expert", axis=0, tiled=True)
    weights = lax.all_gather(gate_weights, "expert", axis=0, tiled=True)
    scale = jnp.sum(
        jnp.where(ids == me, weights.astype(jnp.float32), 0.0), axis=1, keepdims=True
    )
    gated = lax.dot_general(inputs, w_gate[0], contract_last, preferred_element_type=jnp.float32)
    upward = lax.dot_general(inputs, w_up[0], contract_last, preferred_element_type=jnp.float32)
    hidden = (jax.nn.silu(gated) * upward).astype(jnp.bfloat16)
    partial_value = jnp.dot(hidden, w_down[0], preferred_element_type=jnp.float32)
    weighted = (partial_value * scale).astype(jnp.bfloat16)
    across = lax.psum_scatter(weighted, "section", scatter_dimension=1, tiled=True)
    return lax.psum_scatter(across, "expert", scatter_dimension=0, tiled=True)


def solution(mesh):
    placed = (
        P("expert", "section"),
        P("expert", None),
        P("expert", None),
        P("expert", "section", None),
        P("expert", "section", None),
        P("expert", "section", None),
    )
    return jax.shard_map(
        on_device, mesh=mesh, in_specs=placed, out_specs=P("expert", "section"), check_vma=False
    )
```

time: 239 us -> 237 us (level); the launches traced: 237 us -> 233 us
  waiting for transfers between devices: 97 us -> 154 us
  blocking collectives: 94.8 us -> 46.6 us
  starting transfers between devices: 5.41 us -> 0.09 us
  local copies, waits for them, and re-layouts: 3.02 us -> 0.1 us
    all_to_all x1 -> x0, blocking collectives: 88.7 us -> none  [on_device(): lax.all_to_all(send_rows, 'expert', split_axis=0, concat_axis=0, tiled=True)]
    all_to_all x1 -> x0, waiting for transfers between devices: 81 us -> none  [on_device(): lax.all_to_all(partial_value, 'expert', split_axis=0, concat_axis=0, tile...]
    reduce_scatter x0 -> x1, waiting for transfers between devices: none -> 66.8 us  [on_device(): return lax.psum_scatter(across, 'expert', scatter_dimension=0, tiled=True)]
    reduce_scatter x1, waiting for transfers between devices: 16 us -> 67.6 us  [on_device(): lax.psum_scatter(weighted, 'section', scatter_dimension=1, tiled=True)]
    all_gather x1 -> x3, blocking collectives: 6.13 us -> 46.6 us  [the longest x1 22.1 us: on_device(): ids = lax.all_gather(expert_ids, 'expert', axis=0, tiled=True)]
    all_gather x0 -> x1, waiting for transfers between devices: none -> 19.4 us  [on_device(): inputs = lax.all_gather(rows, 'expert', axis=0, tiled=True)]
    dot_general x1, matrix products: 12.2 us -> 4.8 us  [on_device(): jnp.dot(hidden, w_down[0], preferred_element_type=jnp.float32)]
    dot_general x1, matrix products: 2.09 us -> 7.85 us  [on_device(): lax.dot_general(inputs, w_gate[0], contract_last, preferred_element_type=...]
  transfers between devices with their start and end apart: 2 -> 3, of which waited for: 2 -> 3; matrix products, arithmetic and copies ran while one was open for 0% -> 0% of each run, Pallas kernels for 0% -> 0%
where the time goes in v1:
time: 237 us; the launch traced here: 233 us
  waiting for transfers between devices  154 us (65%)
  blocking collectives  46.6 us (20%)
  matrix products  19 us (8%)
  between operations  13.2 us (6%)
    reduce_scatter x1, waiting for transfers between devices, on_device(): lax.psum_scatter(weighted, 'section', scatter_dimension=1, tiled=True)  67.6 us
    reduce_scatter x1, waiting for transfers between devices, on_device(): return lax.psum_scatter(across, 'expert', scatter_dimension=0, tiled=True)  66.8 us
    all_gather x1, blocking collectives, on_device(): ids = lax.all_gather(expert_ids, 'expert', axis=0, tiled=True)  22.1 us
    all_gather x1, waiting for transfers between devices, on_device(): inputs = lax.all_gather(rows, 'expert', axis=0, tiled=True)  19.4 us
    all_gather x1, blocking collectives, on_device(): weights = lax.all_gather(gate_weights, 'expert', axis=0, tiled=True)  16.6 us
    all_gather x1, blocking collectives, on_device(): rows = lax.all_gather(tokens, 'section', axis=1, tiled=True)  7.88 us
    dot_general x1, matrix products, on_device(): lax.dot_general(inputs, w_gate[0], contract_last, preferred_element_type=...  7.85 us
    dot_general x1, matrix products, on_device(): lax.dot_general(inputs, w_up[0], contract_last, preferred_element_type=jn...  6.31 us
  transfers between devices with their start and end apart: 3, of which 3 were waited for; matrix products, arithmetic and copies ran while one was open for 0% of the time, Pallas kernels for 0%

profile of v1, /device:TPU:13, one launch (start us, length us, event | category | flops | bytes accessed | tf_op | source)
XLA Modules:
  0.0 232.8 jit_solution(15738696851114167049)
XLA Ops:
  6.5 0.0 all-gather.4.cloned.1.call-start
  6.5 7.9 %all_gather.12 = bf16[24,7168]{1,0:T(8,128)(2,1)} all-gather(bf16[24,3584]{1,0:T(8,128)(2,1)} %param.6), channel_id=1, replica_groups=mesh['section'=2,'expert'=16] {'section'}, dimensions={1}, use_global_device_ids=true | all-gather | bytes 516096 | tf_op jit(solution)/shard_map/all_gather | solution.py:10
  14.4 0.0 all-gather.4.cloned.1.call-update
  14.4 0.0 reduce-scatter.3.cloned.1.call-start
  14.5 16.6 %all-gather.1 = bf16[16,24,8]{1,2,0:T(8,128)(2,1)S(1)} all-gather(bf16[1,24,8]{1,2,0:T(8,128)(2,1)} %bitcast.19), channel_id=1, replica_groups=mesh['section'=2,'expert'=16] {'expert'}, dimensions={0}, use_global_device_ids=true | all-gather | bytes 6528 | tf_op jit(solution)/shard_map/all_gather | solution.py:13
  31.1 22.1 %all-gather = s32[16,24,8]{1,2,0:T(8,128)S(1)} all-gather(s32[1,24,8]{1,2,0:T(8,128)} %bitcast.18), channel_id=1, replica_groups=mesh['section'=2,'expert'=16] {'expert'}, dimensions={0}, use_global_device_ids=true | all-gather | bytes 13056 | tf_op jit(solution)/shard_map/all_gather | solution.py:12
  53.2 0.1 reshape.10
  53.3 19.4 %all-gather.4.cloned.1.call-done = bf16[384,7168]{1,0:T(8,128)(2,1)} async-done(((bf16[24,7168]{1,0:T(8,128)(2,1)}), bf16[384,7168]{1,0:T(8,128)(2,1)}) %all-gather.4.cloned.1.call-update) | async-done | bytes 5505040 | tf_op jit(solution)/shard_map/all_gather | solution.py:11
  72.7 0.0 copy-start
  72.7 0.0 slice-start
  72.7 7.9 %fusion.3 = f32[384,512]{1,0:T(8,128)S(1)} fusion(bf16[384,7168]{1,0:T(8,128)(2,1)} %all-gather.4.cloned.1.call-done, bf16[1,512,7168]{2,1,0:T(8,128)(2,1)} %param.9), kind=kOutput, calls=%fused_computation.4 | convolution fusion | flops 2818572288 | bytes 13631488 | tf_op jit(solution)/shard_map/dot_general | solution.py:17
  80.6 0.0 copy-done
  80.6 0.0 slice-start.1
  80.6 6.3 %fusion.8 = bf16[384,512]{1,0:T(8,128)(2,1)S(1)} fusion(bf16[384,7168]{1,0:T(8,128)(2,1)S(1)} %copy-done, bf16[1,512,7168]{2,1,0:T(8,128)(2,1)} %param.10, f32[384,512]{1,0:T(8,128)S(1)} %fusion.3), kind=kOutput, calls=%fused_computation.7 | convolution fusion | flops 2819751936 | bytes 14024704 | tf_op jit(solution)/shard_map/dot_general | solution.py:18
  86.9 0.0 slice-done
  86.9 0.0 slice-done.1
  86.9 4.8 %multiply_convert_fusion = bf16[384,7168]{1,0:T(8,128)(2,1)} fusion(bf16[384,512]{1,0:T(8,128)(2,1)S(1)} %fusion.8, bf16[1,512,7168]{2,1,0:T(8,128)(2,1)S(1)} %bitcast.21, f32[384]{0:T(512)S(1)} %reshape.10), kind=kOutput, calls=%fused_computation | convolution fusion | flops 2824077312 | bytes 13239808 | tf_op jit(solution)/shard_map/dot_general | solution.py:20
  91.7 0.0 reduce-scatter.3.cloned.1.call-update
  91.8 0.0 reduce-scatter.5.cloned.1.call-start
  91.8 67.6 %reduce-scatter.3.cloned.1.call-done = bf16[384,3584]{1,0:T(8,128)(2,1)} async-done(((bf16[384,7168]{1,0:T(8,128)(2,1)}), bf16[384,3584]{1,0:T(8,128)(2,1)}) %reduce-scatter.3.cloned.1.call-update) | async-done | bytes 2752528 | tf_op jit(solution)/shard_map/reduce_scatter | solution.py:22
  159.4 0.0 reduce-scatter.5.cloned.1.call-update
  159.4 66.8 %reduce-scatter.5.cloned.1.call-done = bf16[24,3584]{1,0:T(8,128)(2,1)} async-done(((bf16[384,3584]{1,0:T(8,128)(2,1)}), bf16[24,3584]{1,0:T(8,128)(2,1)}) %reduce-scatter.5.cloned.1.call-update) | async-done | bytes 172048 | tf_op jit(solution)/shard_map/reduce_scatter | solution.py:23
  (2 shorter events, 0.0 us)
Async XLA Ops:
  6.5 66.2 %all-gather.4.cloned.1.call-start = ((), (), s32[]{:S(2)}) async-start(), calls=%async_computation.2 | async-start | bytes 5849088 | tf_op jit(solution)/shard_map/all_gather | solution.py:11
  14.4 145.0 %reduce-scatter.3.cloned.1.call-start = ((), (), s32[]{:S(2)}) async-start(), calls=%async_computation.3 | async-start | bytes 8257536 | tf_op jit(solution)/shard_map/reduce_scatter | solution.py:22
  72.7 7.9 %copy-start = (bf16[384,7168]{1,0:T(8,128)(2,1)S(1)}, bf16[384,7168]{1,0:T(8,128)(2,1)}, u32[]{:S(2)}) copy-start(bf16[384,7168]{1,0:T(8,128)(2,1)} %all-gather.4.cloned.1.call-done) | copy-start | bytes 16515076
  72.7 14.2 %slice-start = ((s8[7340032]{0:T(1024)(128)(4,1)}), s8[4194304]{0:T(1024)(128)(4,1)S(1)}, s32[]{:S(2)}) async-start(s8[7340032]{0:T(1024)(128)(4,1)} %bitcast.20), calls=%async_computation.5 | async-start | bytes 8388608
  80.6 6.3 %slice-start.1 = ((s8[7340032]{0:T(1024)(128)(4,1)}), s8[3145728]{0:T(1024)(128)(4,1)S(1)}, s32[]{:S(2)}) async-start(s8[7340032]{0:T(1024)(128)(4,1)} %bitcast.20), calls=%async_computation.6 | async-start | bytes 6291456
  91.8 134.5 %reduce-scatter.5.cloned.1.call-start = ((), (), s32[]{:S(2)}) async-start(), calls=%async_computation.4 | async-start | bytes 2924544 | tf_op jit(solution)/shard_map/reduce_scatter | solution.py:23
Sparse Core Ops, SparseCore 0:
  14.6 58.0 all-gather.3
  91.9 67.4 reduce-scatter.2
  163.7 62.5 reduce-scatter.4

commit v2 on v0

--- a/solution.py
+++ b/solution.py
@@ -1,7 +1,474 @@
+import functools
 import jax
 import jax.numpy as jnp
 from jax import lax
+from jax.experimental import pallas as pl
+from jax.experimental.pallas import tpu as pltpu
 from jax.sharding import PartitionSpec as P
+
+MESH = pl.DeviceIdType.MESH
+F32 = jnp.float32
+BF16 = jnp.bfloat16
+NZ = 4
+N_PAIR = 2 * NZ
+N_DEV = 2 * N_PAIR
+
+
+def moe_kernel(
+    tok_ref, ids_ref, gw_ref, wg_hbm, wu_hbm, wd_hbm, out_ref,
+    wg, wu, wd, rows_x, tok_sib, table, gated, upward, hidden, scale,
+    part, core_out, core_in, first_out, first_in, second_out, second_in,
+    total, line_out, line_in, fin_out, fin_in,
+    sem_w, sem_tok, sem_tab_s, sem_tab_r,
+    sem_line_s, sem_line_r, sem_d1_s, sem_d1_r, sem_d2_s, sem_d2_r, sem_core_s, sem_core_r,
+    sem_cx_s, sem_cx_r, sem_f_s, sem_f_r, sem_s_s, sem_s_r, sem_l_s, sem_l_r, sem_fin,
+):
+    count, _ = tok_ref.shape
+    block = 2 * count
+    chunk = rows_x.shape[2]
+    me = lax.axis_index("expert")
+    x = lax.axis_index("section")
+    z, y, c = me // 4, (me // 2) % 2, me % 2
+
+    def dev(x_, z_, y_, c_):
+        return {"section": x_, "expert": z_ * 4 + y_ * 2 + c_}
+
+    sibling = dev(x, z, y, 1 - c)
+    x_peer = dev(1 - x, z, y, c)
+    y_peer = dev(x, z, 1 - y, c)
+
+    def remote(src, dst, s, r, to):
+        return pltpu.make_async_remote_copy(
+            src_ref=src, dst_ref=dst, send_sem=s, recv_sem=r, device_id=to, device_id_type=MESH
+        )
+
+    weight_copies = [
+        pltpu.make_async_copy(wg_hbm.at[0], wg, sem_w.at[0]),
+        pltpu.make_async_copy(wu_hbm.at[0], wu, sem_w.at[1]),
+        pltpu.make_async_copy(wd_hbm.at[0], wd, sem_w.at[2]),
+    ]
+    for copy in weight_copies:
+        copy.start()
+
+    barrier = pltpu.get_barrier_semaphore()
+    for step in range(1, N_DEV):
+        pl.semaphore_signal(
+            barrier, inc=1, device_id={"section": x, "expert": (me + step) % N_DEV},
+            device_id_type=MESH,
+        )
+    pl.semaphore_signal(barrier, inc=1, device_id=x_peer, device_id_type=MESH)
+    pl.semaphore_wait(barrier, N_DEV)
+
+    tok_copy = remote(tok_ref, tok_sib, sem_tok.at[0], sem_tok.at[1], sibling)
+    tok_copy.start()
+
+    lane = lax.broadcasted_iota(jnp.int32, (count, 128), 1)
+    weights = jnp.zeros((count, 128), F32)
+    for k in range(ids_ref.shape[1]):
+        weights = weights + jnp.where(lane == ids_ref[:, k:k + 1], gw_ref[:, k:k + 1].astype(F32), 0.0)
+    table[me] = weights
+
+    tok_copy.wait()
+    for j in range(4):
+        cols = slice(j * chunk, (j + 1) * chunk)
+        mine, other = tok_ref[:, cols], tok_sib[:, cols]
+        lower = jnp.where(c == 0, mine.astype(F32), other.astype(F32)).astype(BF16)
+        upper = jnp.where(c == 0, other.astype(F32), mine.astype(F32)).astype(BF16)
+        rows_x[x * 4 + j, pl.ds(pl.multiple_of((z * 2 + y) * block, block), block), :] = (
+            jnp.concatenate([lower, upper], axis=0)
+        )
+
+    def spot(h, x_, z_, y_):
+        return rows_x.at[
+            x_ * 4 + c * 2 + h, pl.ds(pl.multiple_of((z_ * 2 + y_) * block, block), block), :
+        ]
+
+    def label(h, x_, z_, y_):
+        return h * 4 * NZ + x_ * N_PAIR + z_ * 2 + y_
+
+    def along_line(h, z_, up):
+        place = spot(h, x, z_, y)
+        to = dev(x, z + 1 if up else z - 1, y, c)
+        return remote(
+            place, place, sem_line_s.at[h * 2 * NZ + (0 if up else NZ) + z_],
+            sem_line_r.at[h * NZ + z_], to,
+        )
+
+    def first_hop(h, z_):
+        place = spot(h, x, z_, y)
+        return remote(
+            place, place, sem_d1_s.at[h * NZ + z_], sem_d1_r.at[h * NZ + z_],
+            y_peer if h == 0 else x_peer,
+        )
+
+    def first_arrived(h, z_):
+        return (h, x, z_, 1 - y) if h == 0 else (h, 1 - x, z_, y)
+
+    def first_wait(h, z_):
+        place = spot(*first_arrived(h, z_))
+        remote(place, place, sem_d1_s.at[h * NZ + z_], sem_d1_r.at[h * NZ + z_], sibling).wait_recv()
+
+    def second_hop(h, z_, own):
+        place = spot(h, x, z_, y) if own else spot(*first_arrived(h, z_))
+        i = h * 2 * NZ + (0 if own else NZ) + z_
+        return remote(
+            place, place, sem_d2_s.at[i], sem_d2_r.at[i], x_peer if h == 0 else y_peer
+        )
+
+    def second_arrived(h, z_, own):
+        if h == 0:
+            return (h, 1 - x, z_, y if own else 1 - y)
+        return (h, x if own else 1 - x, z_, 1 - y)
+
+    def second_wait(h, z_, own):
+        place = spot(*second_arrived(h, z_, own))
+        i = h * 2 * NZ + (0 if own else NZ) + z_
+        remote(place, place, sem_d2_s.at[i], sem_d2_r.at[i], sibling).wait_recv()
+
+    def to_sibling(h, x_, z_, y_):
+        place = spot(h, x_, z_, y_)
+        i = label(h, x_, z_, y_)
+        return remote(place, place, sem_core_s.at[i], sem_core_r.at[i], sibling)
+
+    def from_sibling(h, x_, z_, y_):
+        place = rows_x.at[
+            x_ * 4 + (1 - c) * 2 + h, pl.ds(pl.multiple_of((z_ * 2 + y_) * block, block), block), :
+        ]
+        i = label(h, x_, z_, y_)
+        return remote(place, place, sem_core_s.at[i], sem_core_r.at[i], sibling)
+
+    def level(k, fn):
+        if k == 0:
+            fn(z, None)
+            return
+
+        @pl.when(z - k >= 0)
+        def _():
+            fn(z - k, True)
+
+        @pl.when(z + k < NZ)
+        def _():
+            fn(z + k, False)
+
+    for h in range(2):
+        @pl.when(z < NZ - 1)
+        def _():
+            along_line(h, z, True).start()
+
+        @pl.when(z > 0)
+        def _():
+            along_line(h, z, False).start()
+
+        first_hop(h, z).start()
+        second_hop(h, z, True).start()
+
+    for step in range(1, N_DEV):
+        peer = (me + step) % N_DEV
+        remote(
+            table.at[me], table.at[me], sem_tab_s.at[step], sem_tab_r.at[me],
+            {"section": x, "expert": peer},
+        ).start()
+
+    for k in range(1, NZ + 1):
+        for h in range(2):
+            if k < NZ:
+                def arrived(z_, up):
+                    place = spot(h, x, z_, y)
+                    remote(
+                        place, place, sem_line_s.at[h * 2 * NZ + z_], sem_line_r.at[h * NZ + z_],
+                        sibling,
+                    ).wait_recv()
+                    if up:
+                        @pl.when(z < NZ - 1)
+                        def _():
+                            along_line(h, z_, True).start()
+                    else:
+                        @pl.when(z > 0)
+                        def _():
+                            along_line(h, z_, False).start()
+                    first_hop(h, z_).start()
+                    second_hop(h, z_, True).start()
+                    to_sibling(h, x, z_, y).start()
+
+                level(k, arrived)
+        for h in range(2):
+            def arrived_first(z_, up):
+                first_wait(h, z_)
+                second_hop(h, z_, False).start()
+                to_sibling(*first_arrived(h, z_)).start()
+
+            level(k - 1, arrived_first)
+
+    for own, k in ((True, 0), (True, 1), (False, 0), (True, 2), (False, 1), (True, 3), (False, 2), (False, 3)):
+        for h in range(2):
+            def arrived_second(z_, up):
+                second_wait(h, z_, own)
+                to_sibling(*second_arrived(h, z_, own)).start()
+
+            level(k, arrived_second)
+
+    for h in range(2):
+        for x_ in range(2):
+            for z_ in range(NZ):
+                for y_ in range(2):
+                    @pl.when(jnp.logical_or(x_ != x, jnp.logical_or(z_ != z, y_ != y)))
+                    def _():
+                        from_sibling(h, x_, z_, y_).wait_recv()
+
+    weight_copies[0].wait()
+    weight_copies[1].wait()
+    contract_last = (((1,), (1,)), ((), ()))
+    gated[...] = jnp.zeros_like(gated)
+    upward[...] = jnp.zeros_like(upward)
+
+    def up_step(q, carry):
+        cols = pl.ds(pl.multiple_of(q * chunk, 128), chunk)
+        inputs = rows_x[q]
+        gated[...] += lax.dot_general(inputs, wg[:, cols], contract_last, preferred_element_type=F32)
+        upward[...] += lax.dot_general(inputs, wu[:, cols], contract_last, preferred_element_type=F32)
+        return carry
+
+    lax.fori_loop(0, 8, up_step, 0)
+    value = gated[...]
+    hidden[...] = (value / (1.0 + jnp.exp(-value)) * upward[...]).astype(BF16)
+
+    for step in range(1, N_DEV):
+        peer = (me + N_DEV - step) % N_DEV
+        remote(
+            table.at[peer], table.at[peer], sem_tab_s.at[step], sem_tab_r.at[peer], sibling
+        ).wait_recv()
+    lane = lax.broadcasted_iota(jnp.int32, (N_DEV * count, 128), 1)
+    every = jnp.concatenate([table[i] for i in range(N_DEV)], axis=0)
+    scale[...] = jnp.broadcast_to(
+        jnp.sum(jnp.where(lane == me, every, 0.0), axis=1, keepdims=True), scale.shape
+    )
+
+    weight_copies[2].wait()
+    n_rows = N_PAIR * block
+
+    def down(x_, c_, h):
+        q = x_ * 4 + c_ * 2 + h
+        cols = pl.ds(pl.multiple_of(q * chunk, 128), chunk)
+        return jnp.dot(hidden[...], wd[:, cols], preferred_element_type=F32) * scale[:, 0:1]
+
+    def core_copy(x_, h):
+        i = x_ * 2 + h
+        return remote(core_out.at[i], core_in.at[i], sem_cx_s.at[i], sem_cx_r.at[i], sibling)
+
+    order = ((1 - x, 0), (1 - x, 1), (x, 1), (x, 0))
+
+    def order_step(i):
+        return jnp.where(i < 2, 1 - x, x), jnp.where(jnp.logical_or(i == 1, i == 2), 1, 0)
+
+    def send_step(i, carry):
+        x_, h = order_step(i)
+        core_out[x_ * 2 + h] = down(x_, 1 - c, h).astype(BF16)
+        core_copy(x_, h).start()
+        return carry
+
+    lax.fori_loop(0, 4, send_step, 0)
+
+    def keep_step(i, carry):
+        x_, h = order_step(i)
+        part[x_ * 2 + h] = down(x_, c, h)
+        return carry
+
+    lax.fori_loop(0, 4, keep_step, 0)
+
+    def span(z_, y_):
+        return pl.ds(pl.multiple_of((z_ * 2 + y_) * block, block), block)
+
+    def chip_sum(h, x_, z_, y_):
+        i = x_ * 2 + h
+        return part[i, span(z_, y_), :] + core_in[i, span(z_, y_), :].astype(F32)
+
+    def first_slot(h, other, z_):
+        return h * 2 * NZ + (NZ if other else 0) + z_
+
+    def first_copy(h, other, z_):
+        i = first_slot(h, other, z_)
+        return remote(
+            first_out.at[i], first_in.at[i], sem_f_s.at[i], sem_f_r.at[i],
+            x_peer if h == 0 else y_peer,
+        )
+
+    def second_copy(h, z_):
+        i = h * NZ + z_
+        return remote(
+            second_out.at[i], second_in.at[i], sem_s_s.at[i], sem_s_r.at[i],
+            y_peer if h == 0 else x_peer,
+        )
+
+    zs = range(NZ)
+    for g, (x_, h) in enumerate(order):
+        core_copy(x_, h).wait_recv()
+        if g == 0:
+            for other in (True, False):
+                for z_ in zs:
+                    first_out[first_slot(0, other, z_)] = chip_sum(
+                        0, 1 - x, z_, 1 - y if other else y
+                    ).astype(BF16)
+                    first_copy(0, other, z_).start()
+        elif g in (1, 2):
+            other = g == 1
+            for z_ in zs:
+                first_out[first_slot(1, other, z_)] = chip_sum(
+                    1, 1 - x if other else x, z_, 1 - y
+                ).astype(BF16)
+                first_copy(1, other, z_).start()
+
+    for z_ in zs:
+        for h in range(2):
+            first_copy(h, True, z_).wait_recv()
+            mine = chip_sum(0, x, z_, 1 - y) if h == 0 else chip_sum(1, 1 - x, z_, y)
+            second_out[h * NZ + z_] = (mine + first_in[first_slot(h, True, z_)].astype(F32)).astype(BF16)
+            second_copy(h, z_).start()
+    for z_ in zs:
+        for h in range(2):
+            first_copy(h, False, z_).wait_recv()
+            second_copy(h, z_).wait_recv()
+            total[h * NZ + z_] = (
+                chip_sum(h, x, z_, y)
+                + first_in[first_slot(h, False, z_)].astype(F32)
+                + second_in[h * NZ + z_].astype(F32)
+            )
+
+    near_up = z < NZ // 2
+
+    def line_copy(h, up, dest):
+        i = h * 2 * NZ + up * NZ + dest
+        return remote(
+            line_out.at[i], line_in.at[i], sem_l_s.at[i], sem_l_r.at[i],
+            dev(x, jnp.where(up == 1, z + 1, z - 1), y, c),
+        )
+
+    def line_state(k, turn):
+        up = jnp.where(near_up, 1 - turn, turn)
+        dest = jnp.where(up == 1, NZ - 1 - k, k)
+        active = jnp.where(up == 1, dest - z, z - dest) > 0
+        feeds = jnp.where(up == 1, z, NZ - 1 - z) > 0
+        return up, dest, active, feeds
+
+    for k in range(NZ - 1):
+        for turn in range(2):
+            up, dest, active, feeds = line_state(k, turn)
+
+            @pl.when(jnp.logical_and(active, feeds))
+            def _():
+                for h in range(2):
+                    i = h * 2 * NZ + up * NZ + dest
+                    line_copy(h, up, dest).wait_recv()
+                    line_out[i] = (total[h * NZ + dest] + line_in[i].astype(F32)).astype(BF16)
+                    line_copy(h, up, dest).start()
+
+            @pl.when(jnp.logical_and(active, jnp.logical_not(feeds)))
+            def _():
+                for h in range(2):
+                    i = h * 2 * NZ + up * NZ + dest
+                    line_out[i] = total[h * NZ + dest].astype(BF16)
+                    line_copy(h, up, dest).start()
+
+    for h in range(2):
+        for up in range(2):
+            @pl.when((z > 0) if up == 1 else (z < NZ - 1))
+            def _():
+                line_copy(h, up, z).wait_recv()
+                total[h * NZ + z] += line_in[h * 2 * NZ + up * NZ + z].astype(F32)
+
+    fin_copy = remote(fin_out, fin_in, sem_fin.at[0], sem_fin.at[1], sibling)
+    halves = []
+    for h in range(2):
+        whole = total[h * NZ + z]
+        lower, upper = whole[:count], whole[count:]
+        fin_out[h] = jnp.where(c == 0, upper, lower).astype(BF16)
+        halves.append(jnp.where(c == 0, lower, upper).astype(BF16))
+    fin_copy.start()
+    fin_copy.wait()
+    for h in range(2):
+        theirs = fin_in[h].astype(F32)
+        mine = halves[h].astype(F32)
+        out_ref[:, h * chunk:(h + 1) * chunk] = jnp.where(c == 0, mine, theirs).astype(BF16)
+        out_ref[:, (2 + h) * chunk:(3 + h) * chunk] = jnp.where(c == 0, theirs, mine).astype(BF16)
+
+    for step in range(1, N_DEV):
+        remote(
+            table.at[me], table.at[me], sem_tab_s.at[step], sem_tab_r.at[me], sibling
+        ).wait_send()
+    for h in range(2):
+        for k in range(NZ):
+            def sent(z_, up):
+                if up is None or up:
+                    @pl.when(z < NZ - 1)
+                    def _():
+                        along_line(h, z_, True).wait_send()
+                if not up:
+                    @pl.when(z > 0)
+                    def _():
+                        along_line(h, z_, False).wait_send()
+
+            level(k, sent)
+        for z_ in zs:
+            first_hop(h, z_).wait_send()
+            second_hop(h, z_, True).wait_send()
+            second_hop(h, z_, False).wait_send()
+            for x_ in range(2):
+                for y_ in range(2):
+                    @pl.when(jnp.logical_or(x_ != x, jnp.logical_or(z_ != z, y_ != y)))
+                    def _():
+                        to_sibling(h, x_, z_, y_).wait_send()
+            first_copy(h, True, z_).wait_send()
+            first_copy(h, False, z_).wait_send()
+            second_copy(h, z_).wait_send()
+        for x_ in range(2):
+            core_copy(x_, h).wait_send()
+    for k in range(NZ - 1):
+        for turn in range(2):
+            up, dest, active, feeds = line_state(k, turn)
+
+            @pl.when(active)
+            def _():
+                for h in range(2):
+                    line_copy(h, up, dest).wait_send()
+
+
+def fused(tokens, expert_ids, gate_weights, w_gate, w_up, w_down):
+    count, share = tokens.shape
+    hid, width = w_gate.shape[1:]
+    chunk = share // 4
+    block = 2 * count
+    n_rows = N_PAIR * block
+    dma = pltpu.SemaphoreType.DMA
+    vmem = lambda shape, dtype: pltpu.VMEM(shape, dtype)
+    blocks = lambda n: pltpu.VMEM((n, block, chunk), BF16)
+    return pl.pallas_call(
+        moe_kernel,
+        out_shape=jax.ShapeDtypeStruct((count, share), BF16),
+        in_specs=[pl.BlockSpec(memory_space=pltpu.VMEM)] * 3 + [pl.BlockSpec(memory_space=pl.ANY)] * 3,
+        out_specs=pl.BlockSpec(memory_space=pltpu.VMEM),
+        scratch_shapes=[
+            vmem((hid, width), BF16), vmem((hid, width), BF16), vmem((hid, width), BF16),
+            vmem((8, n_rows, chunk), BF16), vmem((count, share), BF16),
+            vmem((N_DEV, count, 128), F32),
+            vmem((n_rows, hid), F32), vmem((n_rows, hid), F32), vmem((n_rows, hid), BF16),
+            vmem((n_rows, 128), F32),
+            vmem((4, n_rows, chunk), F32), vmem((4, n_rows, chunk), BF16), vmem((4, n_rows, chunk), BF16),
+            blocks(4 * NZ), blocks(4 * NZ), blocks(2 * NZ), blocks(2 * NZ),
+            vmem((2 * NZ, block, chunk), F32), blocks(4 * NZ), blocks(4 * NZ),
+            vmem((2, count, chunk), BF16), vmem((2, count, chunk), BF16),
+            dma((3,)), dma((2,)), dma((N_DEV,)), dma((N_DEV,)),
+            dma((4 * NZ,)), dma((2 * NZ,)), dma((2 * NZ,)), dma((2 * NZ,)),
+            dma((4 * NZ,)), dma((4 * NZ,)), dma((8 * NZ,)), dma((8 * NZ,)),
+            dma((4,)), dma((4,)), dma((4 * NZ,)), dma((4 * NZ,)), dma((2 * NZ,)), dma((2 * NZ,)),
+            dma((4 * NZ,)), dma((4 * NZ,)), dma((2,)),
+        ],
+        compiler_params=pltpu.CompilerParams(
+            collective_id=0, has_side_effects=True, vmem_limit_bytes=60 * 1024 * 1024
+        ),
+        cost_estimate=pl.CostEstimate(
+            flops=6 * n_rows * hid * width, bytes_accessed=6 * hid * width,
+            transcendentals=n_rows * hid,
+        ),
+    )(tokens, expert_ids, gate_weights, w_gate, w_up, w_down)
 
 
 def on_device(tokens, expert_ids, gate_weights, w_gate, w_up, w_down):
@@ -62,6 +529,7 @@
         P("expert", "section", None),
         P("expert", "section", None),
     )
+    whole_kernel = mesh.shape["section"] == 2 and mesh.shape["expert"] == N_DEV
     return jax.shard_map(
-        on_device, mesh=mesh, in_specs=placed, out_specs=P("expert", "section"), check_vma=False
-    )
+        fused if whole_kernel else on_device, mesh=mesh, in_specs=placed, out_specs=P("expert", "section"), check_vma=False
+    )

time: 239 us -> 95.5 us (0.40)
  waiting for transfers between devices: 97 us -> 0 us
  blocking collectives: 94.8 us -> 0 us
  Pallas kernels: 0 us -> 90.7 us
  matrix products: 21.2 us -> 0 us
  between operations: 13.5 us -> 0.01 us
  starting transfers between devices: 5.41 us -> 0 us
  other arithmetic: 2.41 us -> 0 us
    pallas_call x0 -> x1, Pallas kernels: none -> 90.7 us  [fused(): pl.pallas_call(moe_kernel, out_shape=jax.ShapeDtypeStruct((count, share),...]
    all_to_all x1 -> x0, blocking collectives: 88.7 us -> none  [on_device(): lax.all_to_all(send_rows, 'expert', split_axis=0, concat_axis=0, tiled=True)]
    all_to_all x1 -> x0, waiting for transfers between devices: 81 us -> none  [on_device(): lax.all_to_all(partial_value, 'expert', split_axis=0, concat_axis=0, tile...]
    dot_general x4 -> x0, matrix products: 21.2 us -> none  [the longest x1 12.2 us: on_device(): jnp.dot(hidden, w_down[0], preferred_element_type=jnp.float32)]
    reduce_scatter x1 -> x0, waiting for transfers between devices: 16 us -> none  [on_device(): lax.psum_scatter(weighted, 'section', scatter_dimension=1, tiled=True)]
    all_gather x1 -> x0, blocking collectives: 6.13 us -> none  [on_device(): features = lax.all_gather(tokens, 'section', axis=1, tiled=True)]
    all_to_all x1 -> x0, starting transfers between devices: 5.37 us -> none  [on_device(): lax.all_to_all(partial_value, 'expert', split_axis=0, concat_axis=0, tile...]
  transfers between devices with their start and end apart: 2 -> 0, of which waited for: 2 -> 0; matrix products, arithmetic and copies ran while one was open for 0% -> 0% of each run, Pallas kernels for 0% -> 0%
where the time goes in v2:
time: 95.5 us; the launch traced here: 95 us
  Pallas kernels  90.7 us (95%)
  local copies, waits for them, and re-layouts  4.3 us (5%)
    pallas_call x1, Pallas kernels, fused(): pl.pallas_call(moe_kernel, out_shape=jax.ShapeDtypeStruct((count, share),...  90.7 us
    unnamed x3, local copies, waits for them, and re-layouts  4.3 us

profile of v2, /device:TPU:13, one launch (start us, length us, event | category | flops | bytes accessed | tf_op | source)
XLA Modules:
  0.0 95.0 jit_solution(5678073210202872339)
XLA Ops:
  0.0 1.3 %copy.8.gw_ref = bf16[24,8]{1,0:T(8,128)(2,1)} copy(bf16[24,8]{0,1:T(8,128)(2,1)} %param.8) | data formatting | bytes 768 | tf_op args[2]
  1.3 1.4 %copy.7.ids_ref = s32[24,8]{1,0:T(8,128)} copy(s32[24,8]{0,1:T(8,128)} %param.7) | data formatting | bytes 1536 | tf_op args[1]
  2.7 90.7 %shard_map.64 = bf16[24,3584]{1,0:T(8,128)(2,1)} custom-call(bf16[24,3584]{1,0:T(8,128)(2,1)} %tok_ref.1, s32[24,8]{1,0:T(8,128)} %copy.7.ids_ref, bf16[24,8]{1,0:T(8,128)(2,1)} %copy.8.gw_ref, bf16[1,512,7168]{2,1,0:T(8,128)(2,1)} %wg_hbm.1, bf16[1,512,7168]{2,1,0:T(8,128)(2,1)} %wu_hbm.1, bf16[1,512,7168]{2,1,0:T(8,128)(2,1)} %wd_hbm.1), custom_call_target="tpu_custom_call" | custom-call | flops 8455716864 | bytes 22020096 | tf_op jit(solution)/shard_map/pallas_call | solution.py:443
  93.4 1.6 %copy.10 = bf16[24,3584]{1,0:T(8,128)(2,1)} copy(bf16[24,3584]{1,0:T(8,128)(2,1)} %shard_map.64) | data formatting | bytes 344064

commit v3 on v2

--- a/solution.py
+++ b/solution.py
@@ -42,6 +42,9 @@
             src_ref=src, dst_ref=dst, send_sem=s, recv_sem=r, device_id=to, device_id_type=MESH
         )
 
+    def row_at(z_, y_):
+        return pl.ds(pl.multiple_of((y_ * NZ + z_) * block, block), block)
+
     weight_copies = [
         pltpu.make_async_copy(wg_hbm.at[0], wg, sem_w.at[0]),
         pltpu.make_async_copy(wu_hbm.at[0], wu, sem_w.at[1]),
@@ -74,13 +77,13 @@
         mine, other = tok_ref[:, cols], tok_sib[:, cols]
         lower = jnp.where(c == 0, mine.astype(F32), other.astype(F32)).astype(BF16)
         upper = jnp.where(c == 0, other.astype(F32), mine.astype(F32)).astype(BF16)
-        rows_x[x * 4 + j, pl.ds(pl.multiple_of((z * 2 + y) * block, block), block), :] = (
+        rows_x[x * 4 + j, row_at(z, y), :] = (
             jnp.concatenate([lower, upper], axis=0)
         )
 
     def spot(h, x_, z_, y_):
         return rows_x.at[
-            x_ * 4 + c * 2 + h, pl.ds(pl.multiple_of((z_ * 2 + y_) * block, block), block), :
+            x_ * 4 + c * 2 + h, row_at(z_, y_), :
         ]
 
     def label(h, x_, z_, y_):
@@ -132,7 +135,7 @@
 
     def from_sibling(h, x_, z_, y_):
         place = rows_x.at[
-            x_ * 4 + (1 - c) * 2 + h, pl.ds(pl.multiple_of((z_ * 2 + y_) * block, block), block), :
+            x_ * 4 + (1 - c) * 2 + h, row_at(z_, y_), :
         ]
         i = label(h, x_, z_, y_)
         return remote(place, place, sem_core_s.at[i], sem_core_r.at[i], sibling)
@@ -199,36 +202,62 @@
 
             level(k - 1, arrived_first)
 
-    for own, k in ((True, 0), (True, 1), (False, 0), (True, 2), (False, 1), (True, 3), (False, 2), (False, 3)):
-        for h in range(2):
-            def arrived_second(z_, up):
-                second_wait(h, z_, own)
-                to_sibling(*second_arrived(h, z_, own)).start()
-
-            level(k, arrived_second)
-
-    for h in range(2):
-        for x_ in range(2):
-            for z_ in range(NZ):
-                for y_ in range(2):
-                    @pl.when(jnp.logical_or(x_ != x, jnp.logical_or(z_ != z, y_ != y)))
-                    def _():
-                        from_sibling(h, x_, z_, y_).wait_recv()
-
-    weight_copies[0].wait()
-    weight_copies[1].wait()
     contract_last = (((1,), (1,)), ((), ()))
     gated[...] = jnp.zeros_like(gated)
     upward[...] = jnp.zeros_like(upward)
-
-    def up_step(q, carry):
+    weight_copies[0].wait()
+    weight_copies[1].wait()
+    half_rows = NZ * block
+
+    def up_add(q, where):
         cols = pl.ds(pl.multiple_of(q * chunk, 128), chunk)
-        inputs = rows_x[q]
-        gated[...] += lax.dot_general(inputs, wg[:, cols], contract_last, preferred_element_type=F32)
-        upward[...] += lax.dot_general(inputs, wu[:, cols], contract_last, preferred_element_type=F32)
-        return carry
-
-    lax.fori_loop(0, 8, up_step, 0)
+        inputs = rows_x[q, where, :]
+        gated[where, :] += lax.dot_general(inputs, wg[:, cols], contract_last, preferred_element_type=F32)
+        upward[where, :] += lax.dot_general(inputs, wu[:, cols], contract_last, preferred_element_type=F32)
+
+    def up_all_rows(x_):
+        def body(i, carry):
+            up_add(x_ * 4 + i * 2, pl.ds(0, 2 * half_rows))
+            return carry
+
+        lax.fori_loop(0, 2, body, 0)
+
+    def up_half_rows(y_):
+        def body(i, carry):
+            up_add(i * 2 + 1, pl.ds(pl.multiple_of(y_ * half_rows, half_rows), half_rows))
+            return carry
+
+        lax.fori_loop(0, 4, body, 0)
+
+    def wait_sibling(h, x_, y_):
+        for z_ in range(NZ):
+            @pl.when(jnp.logical_or(x_ != x, jnp.logical_or(z_ != z, y_ != y)))
+            def _():
+                from_sibling(h, x_, z_, y_).wait_recv()
+
+    def drain(items):
+        for own, k in items:
+            for h in range(2):
+                def arrived_second(z_, up):
+                    second_wait(h, z_, own)
+                    to_sibling(*second_arrived(h, z_, own)).start()
+
+                level(k, arrived_second)
+
+    for y_ in (y, 1 - y):
+        wait_sibling(0, x, y_)
+    up_all_rows(x)
+    drain(((True, 0), (True, 1), (False, 0), (True, 2)))
+    for x_ in (x, 1 - x):
+        wait_sibling(1, x_, y)
+    up_half_rows(y)
+    drain(((False, 1), (True, 3), (False, 2), (False, 3)))
+    for y_ in (y, 1 - y):
+        wait_sibling(0, 1 - x, y_)
+    up_all_rows(1 - x)
+    for x_ in (x, 1 - x):
+        wait_sibling(1, x_, 1 - y)
+    up_half_rows(1 - y)
     value = gated[...]
     hidden[...] = (value / (1.0 + jnp.exp(-value)) * upward[...]).astype(BF16)
 
@@ -238,7 +267,7 @@
             table.at[peer], table.at[peer], sem_tab_s.at[step], sem_tab_r.at[peer], sibling
         ).wait_recv()
     lane = lax.broadcasted_iota(jnp.int32, (N_DEV * count, 128), 1)
-    every = jnp.concatenate([table[i] for i in range(N_DEV)], axis=0)
+    every = jnp.concatenate([table[z_ * 4 + y_ * 2 + c_] for y_ in range(2) for z_ in range(NZ) for c_ in range(2)], axis=0)
     scale[...] = jnp.broadcast_to(
         jnp.sum(jnp.where(lane == me, every, 0.0), axis=1, keepdims=True), scale.shape
     )
@@ -251,11 +280,17 @@
         cols = pl.ds(pl.multiple_of(q * chunk, 128), chunk)
         return jnp.dot(hidden[...], wd[:, cols], preferred_element_type=F32) * scale[:, 0:1]
 
-    def core_copy(x_, h):
+    def dest_at(j):
+        a, b, d, e = ((3, 3, 0, 0), (2, 0, 3, 1), (1, 2, 1, 2), (0, 1, 2, 3))[j]
+        return jnp.where(z == 0, a, jnp.where(z == 1, b, jnp.where(z == 2, d, e)))
+
+    def core_copy(x_, h, z_, y_):
         i = x_ * 2 + h
-        return remote(core_out.at[i], core_in.at[i], sem_cx_s.at[i], sem_cx_r.at[i], sibling)
-
-    order = ((1 - x, 0), (1 - x, 1), (x, 1), (x, 0))
+        n = i * N_PAIR + z_ * 2 + y_
+        return remote(
+            core_out.at[i, row_at(z_, y_), :], core_in.at[i, row_at(z_, y_), :],
+            sem_cx_s.at[n], sem_cx_r.at[n], sibling,
+        )
 
     def order_step(i):
         return jnp.where(i < 2, 1 - x, x), jnp.where(jnp.logical_or(i == 1, i == 2), 1, 0)
@@ -263,7 +298,9 @@
     def send_step(i, carry):
         x_, h = order_step(i)
         core_out[x_ * 2 + h] = down(x_, 1 - c, h).astype(BF16)
-        core_copy(x_, h).start()
+        for j in range(NZ):
+            for y_ in (1 - y, y):
+                core_copy(x_, h, dest_at(j), y_).start()
         return carry
 
     lax.fori_loop(0, 4, send_step, 0)
@@ -275,12 +312,9 @@
 
     lax.fori_loop(0, 4, keep_step, 0)
 
-    def span(z_, y_):
-        return pl.ds(pl.multiple_of((z_ * 2 + y_) * block, block), block)
-
     def chip_sum(h, x_, z_, y_):
         i = x_ * 2 + h
-        return part[i, span(z_, y_), :] + core_in[i, span(z_, y_), :].astype(F32)
+        return part[i, row_at(z_, y_), :] + core_in[i, row_at(z_, y_), :].astype(F32)
 
     def first_slot(h, other, z_):
         return h * 2 * NZ + (NZ if other else 0) + z_
@@ -300,31 +334,31 @@
         )
 
     zs = range(NZ)
-    for g, (x_, h) in enumerate(order):
-        core_copy(x_, h).wait_recv()
-        if g == 0:
-            for other in (True, False):
-                for z_ in zs:
-                    first_out[first_slot(0, other, z_)] = chip_sum(
-                        0, 1 - x, z_, 1 - y if other else y
-                    ).astype(BF16)
-                    first_copy(0, other, z_).start()
-        elif g in (1, 2):
-            other = g == 1
-            for z_ in zs:
-                first_out[first_slot(1, other, z_)] = chip_sum(
-                    1, 1 - x if other else x, z_, 1 - y
-                ).astype(BF16)
-                first_copy(1, other, z_).start()
-
-    for z_ in zs:
+
+    def first_send(z_):
+        for other in (True, False):
+            y_ = 1 - y if other else y
+            core_copy(1 - x, 0, z_, y_).wait_recv()
+            first_out[first_slot(0, other, z_)] = chip_sum(0, 1 - x, z_, y_).astype(BF16)
+            first_copy(0, other, z_).start()
+            x_ = 1 - x if other else x
+            core_copy(x_, 1, z_, 1 - y).wait_recv()
+            first_out[first_slot(1, other, z_)] = chip_sum(1, x_, z_, 1 - y).astype(BF16)
+            first_copy(1, other, z_).start()
+
+    def second_send(z_):
         for h in range(2):
+            x_, y_ = (x, 1 - y) if h == 0 else (1 - x, y)
+            core_copy(x_, h, z_, y_).wait_recv()
             first_copy(h, True, z_).wait_recv()
-            mine = chip_sum(0, x, z_, 1 - y) if h == 0 else chip_sum(1, 1 - x, z_, y)
-            second_out[h * NZ + z_] = (mine + first_in[first_slot(h, True, z_)].astype(F32)).astype(BF16)
+            second_out[h * NZ + z_] = (
+                chip_sum(h, x_, z_, y_) + first_in[first_slot(h, True, z_)].astype(F32)
+            ).astype(BF16)
             second_copy(h, z_).start()
-    for z_ in zs:
+
+    def gather_total(z_):
         for h in range(2):
+            core_copy(x, h, z_, y).wait_recv()
             first_copy(h, False, z_).wait_recv()
             second_copy(h, z_).wait_recv()
             total[h * NZ + z_] = (
@@ -333,8 +367,6 @@
                 + second_in[h * NZ + z_].astype(F32)
             )
 
-    near_up = z < NZ // 2
-
     def line_copy(h, up, dest):
         i = h * 2 * NZ + up * NZ + dest
         return remote(
@@ -342,31 +374,33 @@
             dev(x, jnp.where(up == 1, z + 1, z - 1), y, c),
         )
 
-    def line_state(k, turn):
-        up = jnp.where(near_up, 1 - turn, turn)
-        dest = jnp.where(up == 1, NZ - 1 - k, k)
-        active = jnp.where(up == 1, dest - z, z - dest) > 0
+    def line_send(j, relayed):
+        dest = dest_at(j)
+        up = jnp.where(dest > z, 1, 0)
         feeds = jnp.where(up == 1, z, NZ - 1 - z) > 0
-        return up, dest, active, feeds
-
-    for k in range(NZ - 1):
-        for turn in range(2):
-            up, dest, active, feeds = line_state(k, turn)
-
-            @pl.when(jnp.logical_and(active, feeds))
-            def _():
-                for h in range(2):
-                    i = h * 2 * NZ + up * NZ + dest
+
+        @pl.when(feeds if relayed else jnp.logical_not(feeds))
+        def _():
+            for h in range(2):
+                i = h * 2 * NZ + up * NZ + dest
+                if relayed:
                     line_copy(h, up, dest).wait_recv()
                     line_out[i] = (total[h * NZ + dest] + line_in[i].astype(F32)).astype(BF16)
-                    line_copy(h, up, dest).start()
-
-            @pl.when(jnp.logical_and(active, jnp.logical_not(feeds)))
-            def _():
-                for h in range(2):
-                    i = h * 2 * NZ + up * NZ + dest
+                else:
                     line_out[i] = total[h * NZ + dest].astype(BF16)
-                    line_copy(h, up, dest).start()
+                line_copy(h, up, dest).start()
+
+    for turn in range(NZ + 3):
+        if turn < NZ:
+            first_send(dest_at(turn))
+        if 0 <= turn - 1 < NZ:
+            second_send(dest_at(turn - 1))
+        if 0 <= turn - 2 < NZ:
+            gather_total(dest_at(turn - 2))
+        if 0 <= turn - 2 < NZ - 1:
+            line_send(turn - 2, False)
+        if 0 <= turn - 3 < NZ - 1:
+            line_send(turn - 3, True)
 
     for h in range(2):
         for up in range(2):
@@ -420,15 +454,13 @@
             first_copy(h, False, z_).wait_send()
             second_copy(h, z_).wait_send()
         for x_ in range(2):
-            core_copy(x_, h).wait_send()
-    for k in range(NZ - 1):
-        for turn in range(2):
-            up, dest, active, feeds = line_state(k, turn)
-
-            @pl.when(active)
-            def _():
-                for h in range(2):
-                    line_copy(h, up, dest).wait_send()
+            for z_ in zs:
+                for y_ in range(2):
+                    core_copy(x_, h, z_, y_).wait_send()
+    for j in range(NZ - 1):
+        dest = dest_at(j)
+        for h in range(2):
+            line_copy(h, jnp.where(dest > z, 1, 0), dest).wait_send()
 
 
 def fused(tokens, expert_ids, gate_weights, w_gate, w_up, w_down):
@@ -458,7 +490,7 @@
             dma((3,)), dma((2,)), dma((N_DEV,)), dma((N_DEV,)),
             dma((4 * NZ,)), dma((2 * NZ,)), dma((2 * NZ,)), dma((2 * NZ,)),
             dma((4 * NZ,)), dma((4 * NZ,)), dma((8 * NZ,)), dma((8 * NZ,)),
-            dma((4,)), dma((4,)), dma((4 * NZ,)), dma((4 * NZ,)), dma((2 * NZ,)), dma((2 * NZ,)),
+            dma((8 * NZ,)), dma((8 * NZ,)), dma((4 * NZ,)), dma((4 * NZ,)), dma((2 * NZ,)), dma((2 * NZ,)),
             dma((4 * NZ,)), dma((4 * NZ,)), dma((2,)),
         ],
         compiler_params=pltpu.CompilerParams(

time: 95.5 us -> 83.9 us (0.88)
  Pallas kernels: 90.7 us -> 79.4 us
    pallas_call x1, Pallas kernels: 90.7 us -> 79.4 us  [fused(): pl.pallas_call(moe_kernel, out_shape=jax.ShapeDtypeStruct((count, share),...]
where the time goes in v3:
time: 83.9 us; the launch traced here: 83.7 us
  Pallas kernels  79.4 us (95%)
  local copies, waits for them, and re-layouts  4.3 us (5%)
    pallas_call x1, Pallas kernels, fused(): pl.pallas_call(moe_kernel, out_shape=jax.ShapeDtypeStruct((count, share),...  79.4 us
    unnamed x3, local copies, waits for them, and re-layouts  4.3 us

profile of v3, /device:TPU:13, one launch (start us, length us, event | category | flops | bytes accessed | tf_op | source)
XLA Modules:
  0.0 83.7 jit_solution(1311469901158575801)
XLA Ops:
  0.0 1.3 %copy.8.gw_ref = bf16[24,8]{1,0:T(8,128)(2,1)} copy(bf16[24,8]{0,1:T(8,128)(2,1)} %param.8) | data formatting | bytes 768 | tf_op args[2]
  1.3 1.4 %copy.7.ids_ref = s32[24,8]{1,0:T(8,128)} copy(s32[24,8]{0,1:T(8,128)} %param.7) | data formatting | bytes 1536 | tf_op args[1]
  2.7 79.4 %shard_map.64 = bf16[24,3584]{1,0:T(8,128)(2,1)} custom-call(bf16[24,3584]{1,0:T(8,128)(2,1)} %tok_ref.1, s32[24,8]{1,0:T(8,128)} %copy.7.ids_ref, bf16[24,8]{1,0:T(8,128)(2,1)} %copy.8.gw_ref, bf16[1,512,7168]{2,1,0:T(8,128)(2,1)} %wg_hbm.1, bf16[1,512,7168]{2,1,0:T(8,128)(2,1)} %wu_hbm.1, bf16[1,512,7168]{2,1,0:T(8,128)(2,1)} %wd_hbm.1), custom_call_target="tpu_custom_call" | custom-call | flops 8455716864 | bytes 22020096 | tf_op jit(solution)/shard_map/pallas_call | solution.py:475
  82.1 1.6 %copy.10 = bf16[24,3584]{1,0:T(8,128)(2,1)} copy(bf16[24,3584]{1,0:T(8,128)(2,1)} %shard_map.64) | data formatting | bytes 344064

commit v4 on v3

--- a/solution.py
+++ b/solution.py
@@ -67,8 +67,10 @@
 
     lane = lax.broadcasted_iota(jnp.int32, (count, 128), 1)
     weights = jnp.zeros((count, 128), F32)
-    for k in range(ids_ref.shape[1]):
-        weights = weights + jnp.where(lane == ids_ref[:, k:k + 1], gw_ref[:, k:k + 1].astype(F32), 0.0)
+    ids = jnp.transpose(ids_ref[...])
+    gains = jnp.transpose(gw_ref[...].astype(F32))
+    for k in range(ids_ref.shape[0]):
+        weights = weights + jnp.where(lane == ids[:, k:k + 1], gains[:, k:k + 1], 0.0)
     table[me] = weights
 
     tok_copy.wait()
@@ -500,7 +502,7 @@
             flops=6 * n_rows * hid * width, bytes_accessed=6 * hid * width,
             transcendentals=n_rows * hid,
         ),
-    )(tokens, expert_ids, gate_weights, w_gate, w_up, w_down)
+    )(tokens, expert_ids.T, gate_weights.T, w_gate, w_up, w_down)
 
 
 def on_device(tokens, expert_ids, gate_weights, w_gate, w_up, w_down):

time: 83.9 us -> 81.2 us (0.968)
  local copies, waits for them, and re-layouts: 4.3 us -> 1.6 us
    unnamed x3 -> x1, local copies, waits for them, and re-layouts: 4.3 us -> 1.6 us
where the time goes in v4:
time: 81.2 us; the launch traced here: 81.1 us
  Pallas kernels  79.4 us (98%)
  local copies, waits for them, and re-layouts  1.6 us (2%)
    pallas_call x1, Pallas kernels, fused(): pl.pallas_call(moe_kernel, out_shape=jax.ShapeDtypeStruct((count, share),...  79.4 us

profile of v4, /device:TPU:13, one launch (start us, length us, event | category | flops | bytes accessed | tf_op | source)
XLA Modules:
  0.0 81.1 jit_solution(16279700177402072616)
XLA Ops:
  0.0 79.4 %shard_map.64 = bf16[24,3584]{1,0:T(8,128)(2,1)} custom-call(bf16[24,3584]{1,0:T(8,128)(2,1)} %tok_ref.1, s32[8,24]{1,0:T(8,128)} %bitcast.2, bf16[8,24]{1,0:T(8,128)(2,1)} %bitcast.3, bf16[1,512,7168]{2,1,0:T(8,128)(2,1)} %wg_hbm.1, bf16[1,512,7168]{2,1,0:T(8,128)(2,1)} %wu_hbm.1, bf16[1,512,7168]{2,1,0:T(8,128)(2,1)} %wd_hbm.1), custom_call_target="tpu_custom_call" | custom-call | flops 8455716864 | bytes 22020096 | tf_op jit(solution)/shard_map/pallas_call | solution.py:477
  79.5 1.6 %copy.8 = bf16[24,3584]{1,0:T(8,128)(2,1)} copy(bf16[24,3584]{1,0:T(8,128)(2,1)} %shard_map.64) | data formatting | bytes 344064

commit v5 on v4

--- a/solution.py
+++ b/solution.py
@@ -60,10 +60,6 @@
             device_id_type=MESH,
         )
     pl.semaphore_signal(barrier, inc=1, device_id=x_peer, device_id_type=MESH)
-    pl.semaphore_wait(barrier, N_DEV)
-
-    tok_copy = remote(tok_ref, tok_sib, sem_tok.at[0], sem_tok.at[1], sibling)
-    tok_copy.start()
 
     lane = lax.broadcasted_iota(jnp.int32, (count, 128), 1)
     weights = jnp.zeros((count, 128), F32)
@@ -72,6 +68,12 @@
     for k in range(ids_ref.shape[0]):
         weights = weights + jnp.where(lane == ids[:, k:k + 1], gains[:, k:k + 1], 0.0)
     table[me] = weights
+    gated[...] = jnp.zeros_like(gated)
+    upward[...] = jnp.zeros_like(upward)
+    pl.semaphore_wait(barrier, N_DEV)
+
+    tok_copy = remote(tok_ref, tok_sib, sem_tok.at[0], sem_tok.at[1], sibling)
+    tok_copy.start()
 
     tok_copy.wait()
     for j in range(4):
@@ -205,8 +207,6 @@
             level(k - 1, arrived_first)
 
     contract_last = (((1,), (1,)), ((), ()))
-    gated[...] = jnp.zeros_like(gated)
-    upward[...] = jnp.zeros_like(upward)
     weight_copies[0].wait()
     weight_copies[1].wait()
     half_rows = NZ * block

time: 81.2 us -> 81.1 us (level)
  no operation moved by 1% of the time
where the time goes in v5:
time: 81.1 us; the launch traced here: 80.9 us
  Pallas kernels  79.3 us (98%)
  local copies, waits for them, and re-layouts  1.6 us (2%)
    pallas_call x1, Pallas kernels, fused(): pl.pallas_call(moe_kernel, out_shape=jax.ShapeDtypeStruct((count, share),...  79.3 us

profile of v5, /device:TPU:13, one launch (start us, length us, event | category | flops | bytes accessed | tf_op | source)
XLA Modules:
  0.0 80.9 jit_solution(9685701607670211784)
XLA Ops:
  0.0 79.3 %shard_map.64 = bf16[24,3584]{1,0:T(8,128)(2,1)} custom-call(bf16[24,3584]{1,0:T(8,128)(2,1)} %tok_ref.1, s32[8,24]{1,0:T(8,128)} %bitcast.2, bf16[8,24]{1,0:T(8,128)(2,1)} %bitcast.3, bf16[1,512,7168]{2,1,0:T(8,128)(2,1)} %wg_hbm.1, bf16[1,512,7168]{2,1,0:T(8,128)(2,1)} %wu_hbm.1, bf16[1,512,7168]{2,1,0:T(8,128)(2,1)} %wd_hbm.1), custom_call_target="tpu_custom_call" | custom-call | flops 8455716864 | bytes 22020096 | tf_op jit(solution)/shard_map/pallas_call | solution.py:477
  79.3 1.6 %copy.8 = bf16[24,3584]{1,0:T(8,128)(2,1)} copy(bf16[24,3584]{1,0:T(8,128)(2,1)} %shard_map.64) | data formatting | bytes 344064
